TPU v7x, 1024 devices: a whole 4x8x16 slice. The times are simulated.
1024 devices in a mesh: wide: 128 (over y, z), narrow: 8 (over x, core).
Axes of the slice: x: 4, y: 8, z: 16, core: 2. Of those that a mesh axis runs over, the one named last changes fastest.
Arguments:
- fine_blocks: bfloat16 [2048, 5, 192, 192], P(('wide', 'narrow')), may hold values from -6 to 6
- prolong_blocks: bfloat16 [2048, 2, 192, 192], P(('wide', 'narrow')), may hold values from -0.4375 to 0.4375
- agg_start: int32 [2048, 2], P(('wide', 'narrow')), may hold values from 0 to 255, as said below
Outputs:
- coarse_blocks: bfloat16 [2048, 17, 192, 192], P(('wide', 'narrow'))
- coarse_numbers: int32 [2048], P(('wide', 'narrow'))
Inputs may be any that keep to these rules, and one draw needn't show every extreme that they name: Along every line of constant second coordinate, aggregates are runs of one or two consecutive pencils, the first pencil of a line always begins one, and the last pencil of the line of second coordinate 0 always begins one. agg_start[i, 0] is the first coordinate of the first pencil of the aggregate holding pencil i; agg_start[i, 1] is that of the aggregate holding the pencil just before i on its line, and equals agg_start[i, 0] at the line's first pencil.
All inputs are finite; a program needn't handle non-finite values.
Results may differ from a plain program's by a relative error of at most 0.0011.
The roundings to bfloat16 on the way count: a program that leaves them out, or rounds other values in their place, can miss the bound.
Values may be sent and summed in bfloat16 or wider, within the bound.
A program may use at most 128 MiB of HBM per device.

v0:
```python
import functools

import jax
import jax.numpy as jnp
from jax import lax
from jax.experimental import pallas as pl
from jax.experimental.pallas import tpu as pltpu
from jax.sharding import PartitionSpec as P

SLOTS = 17
ZDIM = 16
YDIM = 8
NDIM = 8
WDIM = 128
B = 192
W2 = 384
MESH = pl.DeviceIdType.MESH
BF = jnp.bfloat16
F32 = jnp.float32
COUNT_LANE = 4


def pack(x, y):
    lane = lax.broadcasted_iota(jnp.int32, (B, 128), 1)
    xh = jnp.concatenate([x[:, 128:].astype(F32), jnp.zeros((B, 64), F32)], axis=1)
    yh = jnp.concatenate([jnp.zeros((B, 64), F32), y[:, 128:].astype(F32)], axis=1)
    mid = jnp.where(lane < 64, xh, yh).astype(BF)
    return jnp.concatenate([x[:, :128], mid, y[:, :128]], axis=1)


def rows_first(pp):
    return jnp.concatenate([pp, jnp.zeros((64, W2), BF)], axis=0)


def rows_second(pp):
    return jnp.concatenate([jnp.zeros((64, W2), BF), pp[128:], pp[:128]], axis=0)


def mul(a, b):
    return jnp.dot(a, b, preferred_element_type=F32).astype(BF)


def exchange_kernel(
    a_hbm, p_hbm, start_ref,
    prods, pt, ints,
    a_raw, p_raw, pp, pp_up, pp_dn, pp_s, pp_su,
    a_send, a_recv, one_recv, prod_recv,
    own_tile, g1, tile2, r_up2, c_in, c_out, t_in, o_in, g3, o_out,
    local_sem, ssem, rsem, gs, gr, ys, yr, up_ready, low_ready,
):
    w = lax.axis_index("wide")
    n = lax.axis_index("narrow")
    y = w // ZDIM
    z = w % ZDIM
    has_low = w > 0
    has_up = w < WDIM - 1
    low_w = jnp.maximum(w - 1, 0)
    up_w = jnp.minimum(w + 1, WDIM - 1)
    first = z == 0
    last = z == ZDIM - 1
    has_left = n > 0
    has_right = n < NDIM - 1
    left = jnp.maximum(n - 1, 0)
    right = jnp.minimum(n + 1, NDIM - 1)

    load_p = pltpu.make_async_copy(p_hbm, p_raw, local_sem.at[0])
    load_a = pltpu.make_async_copy(a_hbm, a_raw, local_sem.at[1])
    load_p.start()
    load_a.start()

    barrier = pltpu.get_barrier_semaphore()

    def greet(dev):
        pl.semaphore_signal(barrier, inc=1, device_id=dev, device_id_type=MESH)

    @pl.when(z < ZDIM - 1)
    def _():
        greet((up_w, n))

    for d in range(1, NDIM):
        greet((w, lax.rem(n + d, NDIM)))

    @pl.when(first)
    def _():
        for d in range(1, YDIM):
            greet((lax.rem(y + d, YDIM) * ZDIM, n))
        greet((w + ZDIM - 1, n))

    @pl.when(first & has_low)
    def _():
        greet((low_w, n))

    lane = lax.broadcasted_iota(jnp.int32, (8, 128), 1)
    sub = lax.broadcasted_iota(jnp.int32, (8, 128), 0)
    s00, s01, s10, s11 = (start_ref[i, j] for i in range(2) for j in range(2))
    count = (s00 == 2 * w).astype(jnp.int32) + (s10 == 2 * w + 1).astype(jnp.int32)
    tile = jnp.zeros((8, 128), jnp.int32)
    for at, value in enumerate((s00, s01, s10, s11, count)):
        tile = jnp.where(lane == at, value, tile)
    own_tile[...] = tile

    load_p.wait()
    for r in range(2):
        pp[r] = pack(p_raw[r, 0], p_raw[r, 1])

    heard = (
        NDIM - 1
        + jnp.where(first, YDIM - 1, 1)
        + jnp.where(last, 1, 0)
        + jnp.where(last & has_up, 1, 0)
    )
    pl.semaphore_wait(barrier, heard)

    @pl.when(z > 0)
    def _():
        pl.semaphore_signal(up_ready, inc=1, device_id=(low_w, n), device_id_type=MESH)

    @pl.when(last & has_up)
    def _():
        pl.semaphore_signal(low_ready, inc=1, device_id=(up_w, n), device_id_type=MESH)

    def remote(src, dst, at, dev):
        return pltpu.make_async_remote_copy(
            src_ref=src, dst_ref=dst, send_sem=ssem.at[at], recv_sem=rsem.at[at],
            device_id=dev, device_id_type=MESH)

    low, up = (low_w, n), (up_w, n)
    pp_low = remote(pp, pp_up, 0, low)
    pp_high = remote(pp.at[1], pp_dn, 1, up)
    pp_left = remote(pp, pp_s.at[1], 2, (w, left))
    pp_right = remote(pp, pp_s.at[0], 3, (w, right))
    rel_left = remote(pp_up, pp_su.at[1], 4, (w, left))
    rel_right = remote(pp_up, pp_su.at[0], 5, (w, right))
    a_low = [remote(a_send.at[q], a_recv.at[q], 6 + q, low) for q in range(4)]
    one_low = remote(a_raw.at[1, 1], one_recv, 10, low)
    prod_low = remote(prods.at[1, 2], prod_recv, 11, low)
    tile_low = remote(tile2, ints.at[pl.ds(16, 8)], 12, low)
    tile_high = remote(tile2, ints.at[pl.ds(0, 8)], 13, up)
    tile_rel = remote(ints.at[pl.ds(16, 8)], ints.at[pl.ds(24, 8)], 14, low)
    chain_up = remote(c_out, c_in, 15, up)
    chain_wrap = remote(c_out, t_in, 16, (y * ZDIM, n))
    chain_two = remote(o_out, o_in, 17, up)
    gathers = []
    for d in range(1, NDIM):
        gathers.append(pltpu.make_async_remote_copy(
            src_ref=own_tile, dst_ref=g1.at[d], send_sem=gs.at[d], recv_sem=gr.at[d],
            device_id=(w, lax.rem(n + d, NDIM)), device_id_type=MESH))
    totals = []
    for d in range(1, YDIM):
        totals.append(pltpu.make_async_remote_copy(
            src_ref=t_in, dst_ref=g3.at[d], send_sem=ys.at[d], recv_sem=yr.at[d],
            device_id=(lax.rem(y + d, YDIM) * ZDIM, n), device_id_type=MESH))

    for c in gathers:
        c.start()
    pl.when(has_low & ~first)(pp_low.start)
    pl.when(has_left)(pp_left.start)
    pl.when(has_right)(pp_right.start)

    load_a.wait()
    for q, ((i0, k0), (i1, k1)) in enumerate(
        (((0, 0), (0, 1)), ((0, 2), (1, 0)), ((0, 3), (0, 4)), ((1, 3), (1, 4)))):
        a_send[q] = pack(a_raw[i0, k0], a_raw[i1, k1])
        pl.when(has_low & ~first)(a_low[q].start)
    pl.when(has_low & ~first)(one_low.start)

    @pl.when(jnp.logical_not(has_up))
    def _():
        pp_up[...] = jnp.zeros_like(pp_up)
        a_recv[...] = jnp.zeros_like(a_recv)
        one_recv[...] = jnp.zeros_like(one_recv)
        prod_recv[...] = jnp.zeros_like(prod_recv)
        ints[16:32] = jnp.zeros((16, 128), jnp.int32)

    @pl.when(jnp.logical_not(has_low))
    def _():
        pp_dn[...] = jnp.zeros_like(pp_dn)
        ints[0:8] = jnp.zeros((8, 128), jnp.int32)

    for side, there in ((0, has_left), (1, has_right)):
        @pl.when(jnp.logical_not(there))
        def _():
            pp_s[side] = jnp.zeros((2, B, W2), BF)
            pp_su[side] = jnp.zeros((2, B, W2), BF)

    for c in gathers:
        c.wait_recv()
    g1[0] = own_tile[...]
    before = jnp.zeros((8, 128), jnp.int32)
    whole = own_tile[...]
    lines = jnp.where(sub == n, own_tile[...], 0)
    for d in range(1, NDIM):
        piece = g1[d]
        line = lax.rem(n + NDIM - d, NDIM)
        lines = jnp.where(sub == line, piece, lines)
        whole = whole + piece
        before = before + jnp.where(line < n, piece, 0)
    tile2[...] = lines
    ints[8:16] = lines
    pl.when(has_low & ~first)(tile_low.start)

    @pl.when(first)
    def _():
        c_in[...] = jnp.zeros((8, 128), jnp.int32)

    pl.when(z > 0)(chain_up.wait_recv)
    c_out[...] = c_in[...] + whole

    @pl.when(z < ZDIM - 1)
    def _():
        pl.semaphore_wait(up_ready, 1)
        chain_up.start()

    pl.when(last)(chain_wrap.start)
    pl.when(has_up)(tile_high.start)
    pl.when(has_up)(pp_high.start)

    prods[0, 0] = mul(a_raw[0, 0], pp[0])
    prods[0, 2] = mul(a_raw[0, 2], pp[1])
    prods[1, 0] = mul(a_raw[1, 0], pp[1])
    prods[1, 1] = mul(a_raw[1, 1], pp[0])

    def transposed(at, block):
        t = block.astype(F32).T.astype(BF)
        pt[at, 0] = t[:B]
        pt[at, 1] = jnp.concatenate([t[256:], t[B:256]], axis=0)

    for r in range(2):
        transposed(r, pp[r])
    pl.when(has_left)(pp_right.wait_recv)
    for r in range(2):
        prods[r, 3] = mul(a_raw[r, 3], pp_s[0, r])
    pl.when(has_right)(pp_left.wait_recv)
    for r in range(2):
        prods[r, 4] = mul(a_raw[r, 4], pp_s[1, r])

    pl.when(has_up)(pp_low.wait_recv)
    pl.when(has_left)(rel_left.start)
    pl.when(has_right)(rel_right.start)
    prods[1, 2] = mul(a_raw[1, 2], pp_up[0])
    pl.when(has_low & ~first)(prod_low.start)
    pl.when(has_up)(tile_low.wait_recv)
    pl.when(has_low & ~first)(tile_rel.start)
    for r in range(2):
        transposed(2 + r, pp_up[r])

    @pl.when(first & has_low)
    def _():
        pl.semaphore_wait(low_ready, 1)
        pp_low.start()
        for q in range(4):
            a_low[q].start()
        one_low.start()
        prod_low.start()
        tile_low.start()
        tile_rel.start()

    @pl.when(first)
    def _():
        chain_wrap.wait_recv()
        for c in totals:
            c.start()
        for c in totals:
            c.wait_recv()
        offset = jnp.zeros((8, 128), jnp.int32)
        for d in range(1, YDIM):
            offset = offset + jnp.where(lax.rem(y + YDIM - d, YDIM) < y, g3[d], 0)
        o_in[...] = offset
        for c in totals:
            c.wait_send()

    @pl.when(first)
    def _():
        o_out[...] = o_in[...]
        chain_two.start()

    def halo(q, xp, x_at, y_at, yp):
        pl.when(has_up)(a_low[q].wait_recv)
        prods[x_at] = mul(a_recv[q, :, :256], rows_first(xp))
        prods[y_at] = mul(a_recv[q, :, 128:], rows_second(yp))

    halo(0, pp_up[0], (2, 0), (2, 1), pp[1])
    halo(1, pp_up[1], (2, 2), (3, 0), pp_up[1])
    pl.when(has_left)(rel_right.wait_recv)
    pl.when(has_right)(rel_left.wait_recv)
    halo(2, pp_su[0, 0], (2, 3), (2, 4), pp_su[1, 0])
    halo(3, pp_su[0, 1], (3, 3), (3, 4), pp_su[1, 1])
    pl.when(has_low)(pp_high.wait_recv)
    pl.when(has_low)(tile_high.wait_recv)
    prods[0, 1] = mul(a_raw[0, 1], pp_dn[...])
    pl.when(has_up)(one_low.wait_recv)
    prods[3, 1] = mul(one_recv[...], pp_up[0])
    pl.when(has_up)(prod_low.wait_recv)
    prods[3, 2] = prod_recv[...]
    pl.when(has_up)(tile_rel.wait_recv)

    @pl.when(z > 0)
    def _():
        chain_two.wait_recv()
        o_out[...] = o_in[...]

    pl.when((z > 0) & ~last)(chain_two.start)
    ints[32:40] = o_out[...] + c_in[...] + before

    for c in gathers:
        c.wait_send()
    pl.when(has_low)(pp_low.wait_send)
    pl.when(has_up)(pp_high.wait_send)
    pl.when(has_left)(pp_left.wait_send)
    pl.when(has_right)(pp_right.wait_send)
    pl.when(has_left)(rel_left.wait_send)
    pl.when(has_right)(rel_right.wait_send)
    for c in a_low:
        pl.when(has_low)(c.wait_send)
    for c in (one_low, prod_low, tile_low, tile_rel):
        pl.when(has_low)(c.wait_send)
    pl.when(has_up)(tile_high.wait_send)
    pl.when(~last)(chain_up.wait_send)
    pl.when(last)(chain_wrap.wait_send)
    pl.when(~last)(chain_two.wait_send)


def gather_all(fine_blocks, prolong_blocks, agg_start):
    vmem = pl.BlockSpec(memory_space=pltpu.VMEM)
    any_ = pl.BlockSpec(memory_space=pl.ANY)
    i8 = pltpu.VMEM((8, 128), jnp.int32)

    def blocks(*lead):
        return pltpu.VMEM(lead + (B, W2), BF)

    dma = pltpu.SemaphoreType.DMA
    return pl.pallas_call(
        exchange_kernel,
        out_shape=(
            jax.ShapeDtypeStruct((4, 5, B, W2), BF),
            jax.ShapeDtypeStruct((4, 2, B, B), BF),
            jax.ShapeDtypeStruct((40, 128), jnp.int32),
        ),
        in_specs=[any_, any_, pl.BlockSpec(memory_space=pltpu.SMEM)],
        out_specs=(vmem, vmem, vmem),
        scratch_shapes=[
            pltpu.VMEM((2, 5, B, B), BF), pltpu.VMEM((2, 2, B, B), BF),
            blocks(2), blocks(2), blocks(), blocks(2, 2), blocks(2, 2),
            blocks(4), blocks(4), pltpu.VMEM((B, B), BF), blocks(),
            i8, pltpu.VMEM((NDIM, 8, 128), jnp.int32), i8, i8, i8, i8, i8, i8,
            pltpu.VMEM((YDIM, 8, 128), jnp.int32), i8,
            dma((2,)), dma((18,)), dma((18,)), dma((NDIM,)), dma((NDIM,)), dma((YDIM,)), dma((YDIM,)),
            pltpu.SemaphoreType.REGULAR, pltpu.SemaphoreType.REGULAR,
        ],
        compiler_params=pltpu.CompilerParams(
            collective_id=7, has_side_effects=True, vmem_limit_bytes=32 << 20),
    )(fine_blocks, prolong_blocks, agg_start)


def terms_kernel(ints, prods, pt, out, numbers, acc):
    w = lax.axis_index("wide")
    n = lax.axis_index("narrow")
    r = pl.program_id(0)
    row = 2 * w + r

    def start_of(line, rel, q):
        at = rel + 2
        line = jnp.clip(line, 0, NDIM - 1)
        return ints[(at // 2) * 8 + line, (at % 2) * 2 + q]

    begins = start_of(n, r, 0) == row
    other = start_of(n, 0, 0) == 2 * w
    rank = ints[32, COUNT_LANE] + jnp.where((r == 1) & other, 1, 0)
    numbers[r] = jnp.where(begins, rank, -1)

    @pl.when(jnp.logical_not(begins))
    def _():
        out[...] = jnp.zeros_like(out)

    @pl.when(begins)
    def _():
        acc[...] = jnp.zeros_like(acc)
        for ahead, p in ((0, 0), (0, 1), (1, 0), (1, 1), (2, 1)):
            i = r + ahead
            matched = (start_of(n, i, p) == row) & (2 * w + i < 2 * WDIM)

            @pl.when(matched)
            def _():
                @pl.loop(0, 5)
                def _(k):
                    line = n + jnp.where(k == 3, -1, jnp.where(k == 4, 1, 0))
                    rel = i + jnp.where(k == 1, -1, jnp.where(k == 2, 1, 0))
                    x = 2 * w + rel
                    there = (line >= 0) & (line < NDIM) & (x >= 0) & (x < 2 * WDIM)
                    base = jnp.where(k == 3, 9, jnp.where(k == 4, 14, 3)) - row

                    @pl.when(there)
                    def _():
                        term = jnp.dot(pt[i, p], prods[i, k], preferred_element_type=F32)
                        c0 = base + start_of(line, rel, 0)
                        c1 = base + start_of(line, rel, 1)

                        @pl.when((c0 >= 0) & (c0 < SLOTS))
                        def _():
                            acc[c0] += term[:, :B]

                        @pl.when((c1 >= 0) & (c1 < SLOTS))
                        def _():
                            acc[c1, :, :128] += term[:, 256:]
                            acc[c1, :, 128:] += term[:, B:256]

        out[0] = acc[...].astype(BF)


def all_terms(ints, prods, pt):
    whole = lambda *shape: pl.BlockSpec(shape, lambda r: (0,) * len(shape))
    smem = pltpu.SMEM
    return pl.pallas_call(
        terms_kernel,
        grid=(2,),
        out_shape=(
            jax.ShapeDtypeStruct((2, SLOTS, B, B), BF),
            jax.ShapeDtypeStruct((2,), jnp.int32),
        ),
        in_specs=[
            pl.BlockSpec(memory_space=smem),
            pl.BlockSpec(memory_space=pltpu.VMEM),
            pl.BlockSpec(memory_space=pltpu.VMEM),
        ],
        out_specs=(
            pl.BlockSpec((1, SLOTS, B, B), lambda r: (r, 0, 0, 0)),
            pl.BlockSpec(memory_space=smem),
        ),
        scratch_shapes=[pltpu.VMEM((SLOTS, B, B), F32)],
        compiler_params=pltpu.CompilerParams(vmem_limit_bytes=32 << 20),
    )(ints, prods, pt)


def per_device(fine_blocks, prolong_blocks, agg_start):
    prods, pt, ints = gather_all(fine_blocks, prolong_blocks, agg_start)
    return all_terms(ints, prods, pt)


def solution(mesh):
    placed = (
        P(("wide", "narrow"), None, None, None),
        P(("wide", "narrow"), None, None, None),
        P(("wide", "narrow"), None),
    )
    return jax.shard_map(
        per_device,
        mesh=mesh,
        in_specs=placed,
        out_specs=(P(("wide", "narrow"), None, None, None), P(("wide", "narrow"))),
        check_vma=False,
    )
```

profile of v0, /device:TPU:908, one launch (start us, length us, event | category | flops | bytes accessed | tf_op | source)
XLA Modules:
  0.0 109.5 jit_solution(17558679426129377652)
XLA Ops:
  0.6 0.0 copy-start
  0.6 1.2 %copy-done = bf16[2,5,192,192]{3,2,1,0:T(8,128)(2,1)S(1)} copy-done((bf16[2,5,192,192]{3,2,1,0:T(8,128)(2,1)S(1)}, bf16[2,5,192,192]{3,2,1,0:T(8,128)(2,1)}, u32[]{:S(2)}) %copy-start) | copy-done | bytes 737304
  1.8 0.0 copy-start.1
  1.8 1.0 copy-done.1
  2.8 0.0 copy-start.2
  2.8 0.7 copy-done.2
  3.5 93.3 %shard_map.50 = (bf16[4,5,192,384]{3,2,1,0:T(8,128)(2,1)S(1)}, bf16[4,2,192,192]{3,2,1,0:T(8,128)(2,1)S(1)}, s32[40,128]{1,0:T(8,128)S(1)}) custom-call(bf16[2,5,192,192]{3,2,1,0:T(8,128)(2,1)S(1)} %copy-done, bf16[2,2,192,192]{3,2,1,0:T(8,128)(2,1)S(1)} %copy-done.1, s32[2,2]{1,0:T(2,128)S(1)} %copy-done.2), custom_call_target="tpu_custom_call" | custom-call | tf_op jit(solution)/shard_map/pallas_call | solution.py:332
  96.8 12.6 %shard_map.51 = (bf16[2,17,192,192]{3,2,1,0:T(8,128)(2,1)}, s32[2]{0:T(128)}) custom-call(s32[40,128]{1,0:T(8,128)S(1)} %get-tuple-element.5.ints, bf16[4,5,192,384]{3,2,1,0:T(8,128)(2,1)S(1)} %get-tuple-element.6.prods, bf16[4,2,192,192]{3,2,1,0:T(8,128)(2,1)S(1)} %get-tuple-element.7.pt), custom_call_target="tpu_custom_call" | custom-call | tf_op jit(solution)/shard_map/pallas_call | solution.py:413
Async XLA Ops:
  0.6 1.2 %copy-start = (bf16[2,5,192,192]{3,2,1,0:T(8,128)(2,1)S(1)}, bf16[2,5,192,192]{3,2,1,0:T(8,128)(2,1)}, u32[]{:S(2)}) copy-start(bf16[2,5,192,192]{3,2,1,0:T(8,128)(2,1)} %a_hbm.1) | copy-start | bytes 2211844
  1.8 1.0 copy-start.1
  2.8 0.7 copy-start.2
where the time goes:
time: 110 us; the launch traced here: 109 us
  Pallas kernels  106 us (96%)
  local copies, waits for them, and re-layouts  2.87 us (3%)
    pallas_call x1, Pallas kernels, gather_all(): pl.pallas_call(exchange_kernel, out_shape=(jax.ShapeDtypeStruct((4, 5, B,...  93.3 us
    pallas_call x1, Pallas kernels, all_terms(): pl.pallas_call(terms_kernel, grid=(2,), out_shape=(jax.ShapeDtypeStruct((...  12.6 us
    unnamed x6, local copies, waits for them, and re-layouts  2.87 us

commit v1 on v0

v1 whole, which is shorter than its diff:
```python
import functools

import jax
import jax.numpy as jnp
from jax import lax
from jax.experimental import pallas as pl
from jax.experimental.pallas import tpu as pltpu
from jax.sharding import PartitionSpec as P

SLOTS = 17
ZDIM = 16
YDIM = 8
NDIM = 8
WDIM = 128
MID = 7
ROOT = 14
VMEM_LIMIT = 56 << 20
B = 192
W2 = 384
MESH = pl.DeviceIdType.MESH
BF = jnp.bfloat16
F32 = jnp.float32
COUNT_LANE = 4


def pack(x, y):
    lane = lax.broadcasted_iota(jnp.int32, (B, 128), 1)
    xh = jnp.concatenate([x[:, 128:].astype(F32), jnp.zeros((B, 64), F32)], axis=1)
    yh = jnp.concatenate([jnp.zeros((B, 64), F32), y[:, 128:].astype(F32)], axis=1)
    mid = jnp.where(lane < 64, xh, yh).astype(BF)
    return jnp.concatenate([x[:, :128], mid, y[:, :128]], axis=1)


def rows_first(pp):
    return jnp.concatenate([pp, jnp.zeros((64, W2), BF)], axis=0)


def rows_second(pp):
    return jnp.concatenate([jnp.zeros((64, W2), BF), pp[128:], pp[:128]], axis=0)


def mul(a, b):
    return jnp.dot(a, b, preferred_element_type=F32).astype(BF)


def exchange_kernel(
    a_hbm, p_hbm, start_ref,
    prods_hbm, pt_hbm, ints,
    prods, pt, a_raw, p_raw, pp, pp_up, pp_dn, pp_s, pp_su,
    a_send, a_recv, one_recv, prod_recv,
    own_tile, g1, tile2, c_own, g2, t_own, o_in, g3, o_all, c_zero,
    local_sem, out_sem, ssem, rsem, gs, gr, ys, yr, cr, os, up_ready, low_ready, root_ready,
):
    w = lax.axis_index("wide")
    n = lax.axis_index("narrow")
    y = w // ZDIM
    z = w % ZDIM
    has_low = w > 0
    has_up = w < WDIM - 1
    low_w = jnp.maximum(w - 1, 0)
    up_w = jnp.minimum(w + 1, WDIM - 1)
    first = z == 0
    last = z == ZDIM - 1
    root = z == ROOT
    mid = z == MID
    below_mid = (z > 0) & (z < MID)
    root_at = (y * ZDIM + ROOT, n)
    mid_at = (y * ZDIM + MID, n)
    has_left = n > 0
    has_right = n < NDIM - 1
    left = jnp.maximum(n - 1, 0)
    right = jnp.minimum(n + 1, NDIM - 1)

    load_p = pltpu.make_async_copy(p_hbm, p_raw, local_sem.at[0])
    load_a = pltpu.make_async_copy(a_hbm, a_raw, local_sem.at[1])
    load_p.start()
    load_a.start()

    barrier = pltpu.get_barrier_semaphore()

    def greet(dev):
        pl.semaphore_signal(barrier, inc=1, device_id=dev, device_id_type=MESH)

    @pl.when(z < ZDIM - 1)
    def _():
        greet((up_w, n))

    for d in range(1, NDIM):
        greet((w, lax.rem(n + d, NDIM)))

    @pl.when(first & has_low)
    def _():
        greet((low_w, n))

    @pl.when(below_mid & (z < MID - 1))
    def _():
        greet(mid_at)

    @pl.when(z < ROOT - 1)
    def _():
        greet(root_at)

    @pl.when(root)
    def _():
        for d in range(1, YDIM):
            greet((lax.rem(y + d, YDIM) * ZDIM + ROOT, n))

    lane = lax.broadcasted_iota(jnp.int32, (8, 128), 1)
    sub = lax.broadcasted_iota(jnp.int32, (8, 128), 0)
    s00, s01, s10, s11 = (start_ref[i, j] for i in range(2) for j in range(2))
    count = (s00 == 2 * w).astype(jnp.int32) + (s10 == 2 * w + 1).astype(jnp.int32)
    tile = jnp.zeros((8, 128), jnp.int32)
    for at, value in enumerate((s00, s01, s10, s11, count)):
        tile = jnp.where(lane == at, value, tile)
    own_tile[...] = tile

    load_p.wait()
    for r in range(2):
        pp[r] = pack(p_raw[r, 0], p_raw[r, 1])

    heard = (
        NDIM - 1
        + jnp.where(first, 0, 1)
        + jnp.where(mid, MID - 2, 0)
        + jnp.where(root, ROOT - 1 + YDIM - 1, 0)
        + jnp.where(last & has_up, 1, 0)
    )
    pl.semaphore_wait(barrier, heard)

    @pl.when(z > 0)
    def _():
        pl.semaphore_signal(up_ready, inc=1, device_id=(low_w, n), device_id_type=MESH)

    @pl.when(last & has_up)
    def _():
        pl.semaphore_signal(low_ready, inc=1, device_id=(up_w, n), device_id_type=MESH)

    def invite(at):
        pl.semaphore_signal(
            root_ready, inc=1, device_id=(y * ZDIM + at, n), device_id_type=MESH)

    @pl.when(mid)
    def _():
        for at in range(1, MID):
            invite(at)

    @pl.when(root)
    def _():
        for at in range(MID, ROOT):
            invite(at)

    def remote(src, dst, at, dev):
        return pltpu.make_async_remote_copy(
            src_ref=src, dst_ref=dst, send_sem=ssem.at[at], recv_sem=rsem.at[at],
            device_id=dev, device_id_type=MESH)

    low, up = (low_w, n), (up_w, n)
    pp_low = remote(pp, pp_up, 0, low)
    pp_high = remote(pp.at[1], pp_dn, 1, up)
    pp_left = remote(pp, pp_s.at[1], 2, (w, left))
    pp_right = remote(pp, pp_s.at[0], 3, (w, right))
    rel_left = remote(pp_up, pp_su.at[1], 4, (w, left))
    rel_right = remote(pp_up, pp_su.at[0], 5, (w, right))
    a_low = [remote(a_send.at[q], a_recv.at[q], 6 + q, low) for q in range(4)]
    one_low = remote(a_raw.at[1, 1], one_recv, 10, low)
    prod_low = remote(prods.at[1, 2], prod_recv, 11, low)
    tile_low = remote(tile2, ints.at[pl.ds(16, 8)], 12, low)
    tile_high = remote(tile2, ints.at[pl.ds(0, 8)], 13, up)
    tile_rel = remote(ints.at[pl.ds(16, 8)], ints.at[pl.ds(24, 8)], 14, low)
    to_root = pltpu.make_async_remote_copy(
        src_ref=c_own, dst_ref=g2.at[z], send_sem=ssem.at[15], recv_sem=cr.at[z],
        device_id=(y * ZDIM + jnp.where(z < MID, MID, ROOT), n), device_id_type=MESH)
    from_root = remote(o_all.at[0], o_in, 16, root_at)

    zero_root = pltpu.make_async_remote_copy(
        src_ref=c_zero, dst_ref=g2.at[0], send_sem=os.at[0], recv_sem=cr.at[0],
        device_id=mid_at, device_id_type=MESH)

    def reply(at):
        return pltpu.make_async_remote_copy(
            src_ref=o_all.at[at], dst_ref=o_in, send_sem=os.at[at], recv_sem=rsem.at[16],
            device_id=(y * ZDIM + at, n), device_id_type=MESH)

    def arrived(at):
        return pltpu.make_async_remote_copy(
            src_ref=c_own, dst_ref=g2.at[at], send_sem=ssem.at[15], recv_sem=cr.at[at],
            device_id=root_at, device_id_type=MESH)

    others = [at for at in range(ZDIM) if at != ROOT]
    others = others[ROOT:] + others[:ROOT]
    half = pl.ds(0, MID + 1)
    mid_root = pltpu.make_async_remote_copy(
        src_ref=g2.at[half], dst_ref=g2.at[half], send_sem=os.at[0],
        recv_sem=rsem.at[17], device_id=root_at, device_id_type=MESH)

    gathers = []
    for d in range(1, NDIM):
        gathers.append(pltpu.make_async_remote_copy(
            src_ref=own_tile, dst_ref=g1.at[d], send_sem=gs.at[d], recv_sem=gr.at[d],
            device_id=(w, lax.rem(n + d, NDIM)), device_id_type=MESH))
    totals = []
    for d in range(1, YDIM):
        totals.append(pltpu.make_async_remote_copy(
            src_ref=t_own, dst_ref=g3.at[d], send_sem=ys.at[d], recv_sem=yr.at[d],
            device_id=(lax.rem(y + d, YDIM) * ZDIM + ROOT, n), device_id_type=MESH))

    for c in gathers:
        c.start()
    pl.when(has_low & ~first & ~last)(pp_low.start)
    pl.when(has_left)(pp_left.start)
    pl.when(has_right)(pp_right.start)

    load_a.wait()
    for q, ((i0, k0), (i1, k1)) in enumerate(
        (((0, 0), (0, 1)), ((0, 2), (1, 0)), ((0, 3), (0, 4)), ((1, 3), (1, 4)))):
        a_send[q] = pack(a_raw[i0, k0], a_raw[i1, k1])

    @pl.when(jnp.logical_not(has_up))
    def _():
        pp_up[...] = jnp.zeros_like(pp_up)
        a_recv[...] = jnp.zeros_like(a_recv)
        one_recv[...] = jnp.zeros_like(one_recv)
        prod_recv[...] = jnp.zeros_like(prod_recv)
        ints[16:32] = jnp.zeros((16, 128), jnp.int32)

    @pl.when(jnp.logical_not(has_low))
    def _():
        pp_dn[...] = jnp.zeros_like(pp_dn)
        ints[0:8] = jnp.zeros((8, 128), jnp.int32)

    for side, there in ((0, has_left), (1, has_right)):
        @pl.when(jnp.logical_not(there))
        def _():
            pp_s[side] = jnp.zeros((2, B, W2), BF)
            pp_su[side] = jnp.zeros((2, B, W2), BF)

    for c in gathers:
        c.wait_recv()
    g1[0] = own_tile[...]
    before = jnp.zeros((8, 128), jnp.int32)
    whole = own_tile[...]
    lines = jnp.where(sub == n, own_tile[...], 0)
    for d in range(1, NDIM):
        piece = g1[d]
        line = lax.rem(n + NDIM - d, NDIM)
        lines = jnp.where(sub == line, piece, lines)
        whole = whole + piece
        before = before + jnp.where(line < n, piece, 0)
    tile2[...] = lines
    ints[8:16] = lines
    c_own[...] = whole
    pl.when(z > ROOT)(to_root.start)
    pl.when(last)(pp_low.start)

    @pl.when(has_low & ~first)
    def _():
        tile_low.start()
        for q in range(4):
            a_low[q].start()
        one_low.start()

    @pl.when(~last)
    def _():
        pl.semaphore_wait(up_ready, 1)

    pl.when(has_up)(tile_high.start)
    pl.when(has_up)(pp_high.start)

    stores = [
        pltpu.make_async_copy(prods.at[i, k], prods_hbm.at[i, k], out_sem.at[5 * i + k])
        for i in range(4) for k in range(5)]
    stores.append(pltpu.make_async_copy(pt, pt_hbm, out_sem.at[20]))

    def keep(i, k, value):
        prods[i, k] = value
        stores[5 * i + k].start()

    keep(0, 0, mul(a_raw[0, 0], pp[0]))
    keep(0, 2, mul(a_raw[0, 2], pp[1]))
    keep(1, 0, mul(a_raw[1, 0], pp[1]))
    keep(1, 1, mul(a_raw[1, 1], pp[0]))

    def transposed(at, block):
        t = block.astype(F32).T.astype(BF)
        pt[at, 0] = t[:B]
        pt[at, 1] = jnp.concatenate([t[256:], t[B:256]], axis=0)

    for r in range(2):
        transposed(r, pp[r])
    pl.when(has_left)(pp_right.wait_recv)
    for r in range(2):
        keep(r, 3, mul(a_raw[r, 3], pp_s[0, r]))
    pl.when(has_right)(pp_left.wait_recv)
    for r in range(2):
        keep(r, 4, mul(a_raw[r, 4], pp_s[1, r]))

    @pl.when(z == 1)
    def _():
        tile_high.wait_recv()
        c_zero[...] = jnp.broadcast_to(jnp.sum(ints[0:8], axis=0, keepdims=True), (8, 128))

    @pl.when((z > 0) & (z < ROOT))
    def _():
        pl.semaphore_wait(root_ready, 1)

    pl.when((z > 0) & (z < ROOT) & ~mid)(to_root.start)
    pl.when(z == 1)(zero_root.start)

    @pl.when(mid)
    def _():
        g2[MID] = c_own[...]
        for at in range(MID):
            arrived(at).wait_recv()
        mid_root.start()

    @pl.when(root)
    def _():
        g2[ROOT] = c_own[...]
        mid_root.wait_recv()
        for at in range(MID + 1, ZDIM):
            if at != ROOT:
                arrived(at).wait_recv()
        total = jnp.zeros((8, 128), jnp.int32)
        for at in range(ZDIM):
            o_all[at] = total
            total = total + g2[at]
        t_own[...] = total
        for c in totals:
            c.start()
        for c in totals:
            c.wait_recv()
        offset = jnp.zeros((8, 128), jnp.int32)
        for d in range(1, YDIM):
            offset = offset + jnp.where(lax.rem(y + YDIM - d, YDIM) < y, g3[d], 0)
        for at in range(ZDIM):
            o_all[at] = o_all[at] + offset
        o_in[...] = o_all[ROOT]
        for at in others:
            reply(at).start()

    pl.when(has_up)(pp_low.wait_recv)
    pl.when(has_left)(rel_left.start)
    pl.when(has_right)(rel_right.start)
    keep(1, 2, mul(a_raw[1, 2], pp_up[0]))
    pl.when(has_low & ~first)(prod_low.start)
    pl.when(has_up)(tile_low.wait_recv)
    pl.when(has_low & ~first)(tile_rel.start)
    for r in range(2):
        transposed(2 + r, pp_up[r])
    stores[20].start()

    @pl.when(first & has_low)
    def _():
        pl.semaphore_wait(low_ready, 1)
        pp_low.start()
        tile_low.start()
        for q in range(4):
            a_low[q].start()
        one_low.start()
        prod_low.start()
        tile_rel.start()

    def halo(q, xp, x_at, y_at, yp):
        pl.when(has_up)(a_low[q].wait_recv)
        keep(*x_at, mul(a_recv[q, :, :256], rows_first(xp)))
        keep(*y_at, mul(a_recv[q, :, 128:], rows_second(yp)))

    halo(0, pp_up[0], (2, 0), (2, 1), pp[1])
    halo(1, pp_up[1], (2, 2), (3, 0), pp_up[1])
    pl.when(has_left)(rel_right.wait_recv)
    pl.when(has_right)(rel_left.wait_recv)
    halo(2, pp_su[0, 0], (2, 3), (2, 4), pp_su[1, 0])
    halo(3, pp_su[0, 1], (3, 3), (3, 4), pp_su[1, 1])
    pl.when(has_low)(pp_high.wait_recv)
    pl.when(has_low & (z != 1))(tile_high.wait_recv)
    keep(0, 1, mul(a_raw[0, 1], pp_dn[...]))
    pl.when(has_up)(one_low.wait_recv)
    keep(3, 1, mul(one_recv[...], pp_up[0]))
    pl.when(has_up)(prod_low.wait_recv)
    keep(3, 2, prod_recv[...])
    pl.when(has_up)(tile_rel.wait_recv)

    pl.when(~root)(from_root.wait_recv)
    ints[32:40] = o_in[...] + before

    for c in gathers:
        c.wait_send()
    pl.when(has_low)(pp_low.wait_send)
    pl.when(has_up)(pp_high.wait_send)
    pl.when(has_left)(pp_left.wait_send)
    pl.when(has_right)(pp_right.wait_send)
    pl.when(has_left)(rel_left.wait_send)
    pl.when(has_right)(rel_right.wait_send)
    for c in a_low:
        pl.when(has_low)(c.wait_send)
    for c in (one_low, prod_low, tile_low, tile_rel):
        pl.when(has_low)(c.wait_send)
    pl.when(has_up)(tile_high.wait_send)
    pl.when(~root & ~first & ~mid)(to_root.wait_send)
    pl.when(mid)(mid_root.wait_send)
    pl.when(z == 1)(zero_root.wait_send)

    @pl.when(root)
    def _():
        for c in totals:
            c.wait_send()
        for at in others:
            reply(at).wait_send()

    for c in stores:
        c.wait()


def gather_all(fine_blocks, prolong_blocks, agg_start):
    vmem = pl.BlockSpec(memory_space=pltpu.VMEM)
    any_ = pl.BlockSpec(memory_space=pl.ANY)
    i8 = pltpu.VMEM((8, 128), jnp.int32)

    def blocks(*lead):
        return pltpu.VMEM(lead + (B, W2), BF)

    def tiles(count):
        return pltpu.VMEM((count, 8, 128), jnp.int32)

    dma = pltpu.SemaphoreType.DMA
    regular = pltpu.SemaphoreType.REGULAR
    return pl.pallas_call(
        exchange_kernel,
        out_shape=(
            jax.ShapeDtypeStruct((4, 5, B, W2), BF),
            jax.ShapeDtypeStruct((4, 2, B, B), BF),
            jax.ShapeDtypeStruct((40, 128), jnp.int32),
        ),
        in_specs=[any_, any_, pl.BlockSpec(memory_space=pltpu.SMEM)],
        out_specs=(any_, any_, vmem),
        scratch_shapes=[
            blocks(4, 5), pltpu.VMEM((4, 2, B, B), BF),
            pltpu.VMEM((2, 5, B, B), BF), pltpu.VMEM((2, 2, B, B), BF),
            blocks(2), blocks(2), blocks(), blocks(2, 2), blocks(2, 2),
            blocks(4), blocks(4), pltpu.VMEM((B, B), BF), blocks(),
            i8, tiles(NDIM), i8, i8, tiles(ZDIM), i8, i8, tiles(YDIM), tiles(ZDIM), i8,
            dma((2,)), dma((21,)), dma((17,)), dma((18,)), dma((NDIM,)), dma((NDIM,)),
            dma((YDIM,)), dma((YDIM,)), dma((ZDIM,)), dma((ZDIM,)),
            regular, regular, regular,
        ],
        compiler_params=pltpu.CompilerParams(
            collective_id=7, has_side_effects=True, vmem_limit_bytes=VMEM_LIMIT),
    )(fine_blocks, prolong_blocks, agg_start)


def terms_kernel(ints, prods_hbm, pt_hbm, out_hbm, numbers, prods, pt, acc, out, in_sem, out_sem):
    w = lax.axis_index("wide")
    n = lax.axis_index("narrow")
    loads = [
        pltpu.make_async_copy(prods_hbm.at[i], prods.at[i], in_sem.at[i]) for i in range(4)]
    load_pt = pltpu.make_async_copy(pt_hbm, pt, in_sem.at[4])
    load_pt.start()
    for c in loads:
        c.start()

    def start_of(line, rel, q):
        at = rel + 2
        line = jnp.clip(line, 0, NDIM - 1)
        return ints[(at // 2) * 8 + line, (at % 2) * 2 + q]

    other = start_of(n, 0, 0) == 2 * w
    for r in range(2):
        row = 2 * w + r
        begins = start_of(n, r, 0) == row
        rank = ints[32, COUNT_LANE]
        if r == 1:
            rank = rank + jnp.where(other, 1, 0)
        numbers[r] = jnp.where(begins, rank, -1)

        def add(i, columns, row=row, r=r):
            for k in range(5):
                line = n + (0, 0, 0, -1, 1)[k]
                rel = i + (0, -1, 1, 0, 0)[k]
                x = 2 * w + rel
                there = (line >= 0) & (line < NDIM) & (x >= 0) & (x < 2 * WDIM)
                base = (3, 3, 3, 9, 14)[k] - row
                slots = []
                for q in range(2):
                    c = base + start_of(line, rel, q)
                    slots.append(jnp.where(there & (c >= 0) & (c < SLOTS), c, SLOTS))
                term = sum(
                    jnp.dot(pt[i, p], prods[i, k], preferred_element_type=F32)
                    for p in columns)
                acc[r, slots[0]] += term[:, :B]
                acc[r, slots[1], :, :128] += term[:, 256:]
                acc[r, slots[1], :, 128:] += term[:, B:256]

        acc[r] = jnp.zeros((SLOTS + 1, B, B), F32)
        if r == 0:
            load_pt.wait()
        for ahead in range(3):
            i = r + ahead
            if r == 0 or ahead == 2:
                loads[i].wait()
            inside = begins & (2 * w + i < 2 * WDIM)
            first = inside & (start_of(n, i, 0) == row)
            second = inside & (start_of(n, i, 1) == row)
            if ahead == 2:
                pl.when(second)(functools.partial(add, i, (1,)))
            else:
                pl.when(first & second)(functools.partial(add, i, (0, 1)))
                pl.when(first & ~second)(functools.partial(add, i, (0,)))
                pl.when(second & ~first)(functools.partial(add, i, (1,)))
        out[r] = acc[r, :SLOTS].astype(BF)
        pltpu.make_async_copy(out.at[r], out_hbm.at[r], out_sem.at[r]).start()
    for r in range(2):
        pltpu.make_async_copy(out.at[r], out_hbm.at[r], out_sem.at[r]).wait()


def all_terms(ints, prods, pt):
    any_ = pl.BlockSpec(memory_space=pl.ANY)
    smem = pl.BlockSpec(memory_space=pltpu.SMEM)
    return pl.pallas_call(
        terms_kernel,
        out_shape=(
            jax.ShapeDtypeStruct((2, SLOTS, B, B), BF),
            jax.ShapeDtypeStruct((2,), jnp.int32),
        ),
        in_specs=[smem, any_, any_],
        out_specs=(any_, smem),
        scratch_shapes=[
            pltpu.VMEM((4, 5, B, W2), BF), pltpu.VMEM((4, 2, B, B), BF),
            pltpu.VMEM((2, SLOTS + 1, B, B), F32), pltpu.VMEM((2, SLOTS, B, B), BF),
            pltpu.SemaphoreType.DMA((5,)), pltpu.SemaphoreType.DMA((2,)),
        ],
        compiler_params=pltpu.CompilerParams(vmem_limit_bytes=VMEM_LIMIT),
    )(ints, prods, pt)


def per_device(fine_blocks, prolong_blocks, agg_start):
    prods, pt, ints = gather_all(fine_blocks, prolong_blocks, agg_start)
    return all_terms(ints, prods, pt)


def solution(mesh):
    placed = (
        P(("wide", "narrow"), None, None, None),
        P(("wide", "narrow"), None, None, None),
        P(("wide", "narrow"), None),
    )
    return jax.shard_map(
        per_device,
        mesh=mesh,
        in_specs=placed,
        out_specs=(P(("wide", "narrow"), None, None, None), P(("wide", "narrow"))),
        check_vma=False,
    )
```

time: 110 us -> 55.7 us (0.51)
  the two profiles are of different devices: /device:TPU:908 before, /device:TPU:56 now
where the time goes in v1:
time: 55.7 us; the launch traced here: 55.4 us
  Pallas kernels  54.8 us (98%)
  between operations  0.64 us (1%)
    pallas_call x1, Pallas kernels, gather_all(): pl.pallas_call(exchange_kernel, out_shape=(jax.ShapeDtypeStruct((4, 5, B,...  48 us
    pallas_call x1, Pallas kernels, all_terms(): pl.pallas_call(terms_kernel, out_shape=(jax.ShapeDtypeStruct((2, SLOTS, B...  6.76 us

profile of v1, /device:TPU:56, one launch (start us, length us, event | category | flops | bytes accessed | tf_op | source)
XLA Modules:
  0.0 55.4 jit_solution(8970182868533137468)
XLA Ops:
  0.6 48.0 %shard_map.50 = (bf16[4,5,192,384]{3,2,1,0:T(8,128)(2,1)}, bf16[4,2,192,192]{3,2,1,0:T(8,128)(2,1)}, s32[40,128]{1,0:T(8,128)}) custom-call(bf16[2,5,192,192]{3,2,1,0:T(8,128)(2,1)} %a_hbm.1, bf16[2,2,192,192]{3,2,1,0:T(8,128)(2,1)} %p_hbm.1, s32[2,2]{1,0:T(2,128)} %start_ref.1), custom_call_target="tpu_custom_call" | custom-call | tf_op jit(solution)/shard_map/pallas_call | solution.py:427
  48.6 6.8 %shard_map.51 = (bf16[2,17,192,192]{3,2,1,0:T(8,128)(2,1)}, s32[2]{0:T(128)}) custom-call(s32[40,128]{1,0:T(8,128)} %get-tuple-element.5.ints, bf16[4,5,192,384]{3,2,1,0:T(8,128)(2,1)} %get-tuple-element.6.prods_hbm, bf16[4,2,192,192]{3,2,1,0:T(8,128)(2,1)} %get-tuple-element.7.pt_hbm), custom_call_target="tpu_custom_call" | custom-call | tf_op jit(solution)/shard_map/pallas_call | solution.py:518

commit v2 on v1

--- a/solution.py
+++ b/solution.py
@@ -45,8 +45,8 @@
 
 def exchange_kernel(
     a_hbm, p_hbm, start_ref,
-    prods_hbm, pt_hbm, ints,
-    prods, pt, a_raw, p_raw, pp, pp_up, pp_dn, pp_s, pp_su,
+    out_hbm, numbers,
+    ints, prods, pt, acc, out, rank_tile, rank_smem, a_raw, p_raw, pp, pp_up, pp_dn, pp_s, pp_su,
     a_send, a_recv, one_recv, prod_recv,
     own_tile, g1, tile2, c_own, g2, t_own, o_in, g3, o_all, c_zero,
     local_sem, out_sem, ssem, rsem, gs, gr, ys, yr, cr, os, up_ready, low_ready, root_ready,
@@ -114,10 +114,6 @@
         tile = jnp.where(lane == at, value, tile)
     own_tile[...] = tile
 
-    load_p.wait()
-    for r in range(2):
-        pp[r] = pack(p_raw[r, 0], p_raw[r, 1])
-
     heard = (
         NDIM - 1
         + jnp.where(first, 0, 1)
@@ -148,6 +144,10 @@
     def _():
         for at in range(MID, ROOT):
             invite(at)
+
+    load_p.wait()
+    for r in range(2):
+        pp[r] = pack(p_raw[r, 0], p_raw[r, 1])
 
     def remote(src, dst, at, dev):
         return pltpu.make_async_remote_copy(
@@ -266,14 +266,8 @@
     pl.when(has_up)(tile_high.start)
     pl.when(has_up)(pp_high.start)
 
-    stores = [
-        pltpu.make_async_copy(prods.at[i, k], prods_hbm.at[i, k], out_sem.at[5 * i + k])
-        for i in range(4) for k in range(5)]
-    stores.append(pltpu.make_async_copy(pt, pt_hbm, out_sem.at[20]))
-
     def keep(i, k, value):
         prods[i, k] = value
-        stores[5 * i + k].start()
 
     keep(0, 0, mul(a_raw[0, 0], pp[0]))
     keep(0, 2, mul(a_raw[0, 2], pp[1]))
@@ -347,7 +341,6 @@
     pl.when(has_low & ~first)(tile_rel.start)
     for r in range(2):
         transposed(2 + r, pp_up[r])
-    stores[20].start()
 
     @pl.when(first & has_low)
     def _():
@@ -380,8 +373,65 @@
     keep(3, 2, prod_recv[...])
     pl.when(has_up)(tile_rel.wait_recv)
 
+    def start_of(line, rel, q):
+        tile = ints[(rel + 2) // 2 * 8:(rel + 2) // 2 * 8 + 8]
+        at = (rel % 2) * 2 + q
+        chosen = jnp.where((sub == line) & (lane == at), tile, 0)
+        return jnp.sum(jnp.sum(chosen, axis=1, keepdims=True), axis=0, keepdims=True)
+
+    starts = {}
+    for rel in range(-1, 5):
+        for side in (-1, 0, 1) if 0 <= rel < 4 else (0,):
+            for q in range(2):
+                starts[rel, side, q] = start_of(n + side, rel, q)
+
+    stores = []
+    for r in range(2):
+        acc[...] = jnp.zeros_like(acc)
+        for ahead in range(3):
+            i = r + ahead
+            inside = 2 * w + i < 2 * WDIM
+            left_sides = []
+            for p in (1,) if ahead == 2 else (0, 1):
+                mine = (starts[i, 0, p] == 2 * w + r) & inside
+                chosen = jnp.where(mine, pt[i, p].astype(F32), 0.0).astype(BF)
+                left_sides.append(chosen)
+            for k in range(5):
+                side = (0, 0, 0, -1, 1)[k]
+                rel = i + (0, -1, 1, 0, 0)[k]
+                x = 2 * w + rel
+                there = (n + side >= 0) & (n + side < NDIM) & (x >= 0) & (x < 2 * WDIM)
+                term = sum(
+                    jnp.dot(c, prods[i, k], preferred_element_type=F32) for c in left_sides)
+
+                def put(q, shift, r=r, k=k, rel=rel, there=there, term=term, side=side, x=x):
+                    slot = (3, 3, 3, 9, 14)[k] + rel + shift - r
+                    here = (starts[rel, side, q] == x + shift) & there
+                    if q == 0:
+                        acc[slot] += jnp.where(here, term[:, :B], 0.0)
+                    else:
+                        acc[slot, :, :128] += jnp.where(here, term[:, 256:], 0.0)
+                        acc[slot, :, 128:] += jnp.where(here, term[:, B:256], 0.0)
+
+                put(0, 0)
+                put(0, -1)
+                put(1, -1)
+                put(1, -2)
+                if rel == 0:
+                    pl.when(w == 0)(functools.partial(put, 1, 0))
+        out[r] = acc[...].astype(BF)
+        stores.append(pltpu.make_async_copy(out.at[r], out_hbm.at[r], out_sem.at[r]))
+        stores[r].start()
+
     pl.when(~root)(from_root.wait_recv)
-    ints[32:40] = o_in[...] + before
+    rank_tile[...] = o_in[...] + before
+    ranks = pltpu.make_async_copy(rank_tile, rank_smem, local_sem.at[0])
+    ranks.start()
+    ranks.wait()
+    rank = rank_smem[0, COUNT_LANE]
+    begins = s00 == 2 * w
+    numbers[0] = jnp.where(begins, rank, -1)
+    numbers[1] = jnp.where(s10 == 2 * w + 1, rank + jnp.where(begins, 1, 0), -1)
 
     for c in gathers:
         c.wait_send()
@@ -412,7 +462,7 @@
 
 
 def gather_all(fine_blocks, prolong_blocks, agg_start):
-    vmem = pl.BlockSpec(memory_space=pltpu.VMEM)
+    smem = pl.BlockSpec(memory_space=pltpu.SMEM)
     any_ = pl.BlockSpec(memory_space=pl.ANY)
     i8 = pltpu.VMEM((8, 128), jnp.int32)
 
@@ -427,19 +477,21 @@
     return pl.pallas_call(
         exchange_kernel,
         out_shape=(
-            jax.ShapeDtypeStruct((4, 5, B, W2), BF),
-            jax.ShapeDtypeStruct((4, 2, B, B), BF),
-            jax.ShapeDtypeStruct((40, 128), jnp.int32),
+            jax.ShapeDtypeStruct((2, SLOTS, B, B), BF),
+            jax.ShapeDtypeStruct((2,), jnp.int32),
         ),
-        in_specs=[any_, any_, pl.BlockSpec(memory_space=pltpu.SMEM)],
-        out_specs=(any_, any_, vmem),
+        in_specs=[any_, any_, smem],
+        out_specs=(any_, smem),
         scratch_shapes=[
+            pltpu.VMEM((32, 128), jnp.int32),
             blocks(4, 5), pltpu.VMEM((4, 2, B, B), BF),
+            pltpu.VMEM((SLOTS, B, B), F32), pltpu.VMEM((2, SLOTS, B, B), BF),
+            i8, pltpu.SMEM((8, 128), jnp.int32),
             pltpu.VMEM((2, 5, B, B), BF), pltpu.VMEM((2, 2, B, B), BF),
             blocks(2), blocks(2), blocks(), blocks(2, 2), blocks(2, 2),
             blocks(4), blocks(4), pltpu.VMEM((B, B), BF), blocks(),
             i8, tiles(NDIM), i8, i8, tiles(ZDIM), i8, i8, tiles(YDIM), tiles(ZDIM), i8,
-            dma((2,)), dma((21,)), dma((17,)), dma((18,)), dma((NDIM,)), dma((NDIM,)),
+            dma((2,)), dma((2,)), dma((17,)), dma((18,)), dma((NDIM,)), dma((NDIM,)),
             dma((YDIM,)), dma((YDIM,)), dma((ZDIM,)), dma((ZDIM,)),
             regular, regular, regular,
         ],
@@ -448,93 +500,50 @@
     )(fine_blocks, prolong_blocks, agg_start)
 
 
-def terms_kernel(ints, prods_hbm, pt_hbm, out_hbm, numbers, prods, pt, acc, out, in_sem, out_sem):
-    w = lax.axis_index("wide")
-    n = lax.axis_index("narrow")
-    loads = [
-        pltpu.make_async_copy(prods_hbm.at[i], prods.at[i], in_sem.at[i]) for i in range(4)]
-    load_pt = pltpu.make_async_copy(pt_hbm, pt, in_sem.at[4])
-    load_pt.start()
-    for c in loads:
+def hand_over_kernel(blocks_hbm, numbers_hbm, out_hbm, out_numbers, held, in_sem, out_sem):
+    copies = [(r, slice(at, min(at + 3, SLOTS))) for r in range(2) for at in range(0, SLOTS, 3)]
+    small = pltpu.make_async_copy(numbers_hbm, out_numbers, in_sem.at[len(copies)])
+    small.start()
+    reads = [
+        pltpu.make_async_copy(
+            blocks_hbm.at[r, pl.ds(at.start, at.stop - at.start)],
+            held.at[r, pl.ds(at.start, at.stop - at.start)], in_sem.at[c])
+        for c, (r, at) in enumerate(copies)]
+    writes = [
+        pltpu.make_async_copy(
+            held.at[r, pl.ds(at.start, at.stop - at.start)],
+            out_hbm.at[r, pl.ds(at.start, at.stop - at.start)], out_sem.at[c])
+        for c, (r, at) in enumerate(copies)]
+    for c in reads:
         c.start()
-
-    def start_of(line, rel, q):
-        at = rel + 2
-        line = jnp.clip(line, 0, NDIM - 1)
-        return ints[(at // 2) * 8 + line, (at % 2) * 2 + q]
-
-    other = start_of(n, 0, 0) == 2 * w
-    for r in range(2):
-        row = 2 * w + r
-        begins = start_of(n, r, 0) == row
-        rank = ints[32, COUNT_LANE]
-        if r == 1:
-            rank = rank + jnp.where(other, 1, 0)
-        numbers[r] = jnp.where(begins, rank, -1)
-
-        def add(i, columns, row=row, r=r):
-            for k in range(5):
-                line = n + (0, 0, 0, -1, 1)[k]
-                rel = i + (0, -1, 1, 0, 0)[k]
-                x = 2 * w + rel
-                there = (line >= 0) & (line < NDIM) & (x >= 0) & (x < 2 * WDIM)
-                base = (3, 3, 3, 9, 14)[k] - row
-                slots = []
-                for q in range(2):
-                    c = base + start_of(line, rel, q)
-                    slots.append(jnp.where(there & (c >= 0) & (c < SLOTS), c, SLOTS))
-                term = sum(
-                    jnp.dot(pt[i, p], prods[i, k], preferred_element_type=F32)
-                    for p in columns)
-                acc[r, slots[0]] += term[:, :B]
-                acc[r, slots[1], :, :128] += term[:, 256:]
-                acc[r, slots[1], :, 128:] += term[:, B:256]
-
-        acc[r] = jnp.zeros((SLOTS + 1, B, B), F32)
-        if r == 0:
-            load_pt.wait()
-        for ahead in range(3):
-            i = r + ahead
-            if r == 0 or ahead == 2:
-                loads[i].wait()
-            inside = begins & (2 * w + i < 2 * WDIM)
-            first = inside & (start_of(n, i, 0) == row)
-            second = inside & (start_of(n, i, 1) == row)
-            if ahead == 2:
-                pl.when(second)(functools.partial(add, i, (1,)))
-            else:
-                pl.when(first & second)(functools.partial(add, i, (0, 1)))
-                pl.when(first & ~second)(functools.partial(add, i, (0,)))
-                pl.when(second & ~first)(functools.partial(add, i, (1,)))
-        out[r] = acc[r, :SLOTS].astype(BF)
-        pltpu.make_async_copy(out.at[r], out_hbm.at[r], out_sem.at[r]).start()
-    for r in range(2):
-        pltpu.make_async_copy(out.at[r], out_hbm.at[r], out_sem.at[r]).wait()
-
-
-def all_terms(ints, prods, pt):
+    for before, after in zip(reads, writes):
+        before.wait()
+        after.start()
+    for c in writes:
+        c.wait()
+    small.wait()
+
+
+def hand_over(blocks, numbers):
     any_ = pl.BlockSpec(memory_space=pl.ANY)
-    smem = pl.BlockSpec(memory_space=pltpu.SMEM)
     return pl.pallas_call(
-        terms_kernel,
+        hand_over_kernel,
         out_shape=(
-            jax.ShapeDtypeStruct((2, SLOTS, B, B), BF),
-            jax.ShapeDtypeStruct((2,), jnp.int32),
+            jax.ShapeDtypeStruct(blocks.shape, blocks.dtype),
+            jax.ShapeDtypeStruct(numbers.shape, numbers.dtype),
         ),
-        in_specs=[smem, any_, any_],
-        out_specs=(any_, smem),
+        in_specs=[any_, any_],
+        out_specs=(any_, any_),
         scratch_shapes=[
-            pltpu.VMEM((4, 5, B, W2), BF), pltpu.VMEM((4, 2, B, B), BF),
-            pltpu.VMEM((2, SLOTS + 1, B, B), F32), pltpu.VMEM((2, SLOTS, B, B), BF),
-            pltpu.SemaphoreType.DMA((5,)), pltpu.SemaphoreType.DMA((2,)),
+            pltpu.VMEM((2, SLOTS, B, B), BF),
+            pltpu.SemaphoreType.DMA((13,)), pltpu.SemaphoreType.DMA((12,)),
         ],
         compiler_params=pltpu.CompilerParams(vmem_limit_bytes=VMEM_LIMIT),
-    )(ints, prods, pt)
+    )(blocks, numbers)
 
 
 def per_device(fine_blocks, prolong_blocks, agg_start):
-    prods, pt, ints = gather_all(fine_blocks, prolong_blocks, agg_start)
-    return all_terms(ints, prods, pt)
+    return hand_over(*gather_all(fine_blocks, prolong_blocks, agg_start))
 
 
 def solution(mesh):

time: 55.7 us -> 51.5 us (0.925)
  Pallas kernels: 54.8 us -> 50.6 us
    pallas_call x2, Pallas kernels: 54.8 us -> 50.6 us  [the longest x1 47.7 us: gather_all(): pl.pallas_call(exchange_kernel, out_shape=(jax.ShapeDtypeStruct((2, SLOTS...]
where the time goes in v2:
time: 51.5 us; the launch traced here: 51.3 us
  Pallas kernels  50.6 us (98%)
  between operations  0.64 us (1%)
    pallas_call x1, Pallas kernels, gather_all(): pl.pallas_call(exchange_kernel, out_shape=(jax.ShapeDtypeStruct((2, SLOTS...  47.7 us
    pallas_call x1, Pallas kernels, hand_over(): pl.pallas_call(hand_over_kernel, out_shape=(jax.ShapeDtypeStruct(blocks.s...  2.9 us

profile of v2, /device:TPU:56, one launch (start us, length us, event | category | flops | bytes accessed | tf_op | source)
XLA Modules:
  0.0 51.3 jit_solution(2461714810237307026)
XLA Ops:
  0.6 47.7 %shard_map.50 = (bf16[2,17,192,192]{3,2,1,0:T(8,128)(2,1)}, s32[2]{0:T(128)}) custom-call(bf16[2,5,192,192]{3,2,1,0:T(8,128)(2,1)} %a_hbm.1, bf16[2,2,192,192]{3,2,1,0:T(8,128)(2,1)} %p_hbm.1, s32[2,2]{1,0:T(2,128)} %start_ref.1), custom_call_target="tpu_custom_call" | custom-call | tf_op jit(solution)/shard_map/pallas_call | solution.py:477
  48.4 2.9 %shard_map.51 = (bf16[2,17,192,192]{3,2,1,0:T(8,128)(2,1)}, s32[2]{0:T(128)}) custom-call(bf16[2,17,192,192]{3,2,1,0:T(8,128)(2,1)} %get-tuple-element.4.blocks_hbm, s32[2]{0:T(128)} %get-tuple-element.5.numbers_hbm), custom_call_target="tpu_custom_call" | custom-call | tf_op jit(solution)/shard_map/pallas_call | solution.py:529

commit v3 on v2

--- a/solution.py
+++ b/solution.py
@@ -266,6 +266,15 @@
     pl.when(has_up)(tile_high.start)
     pl.when(has_up)(pp_high.start)
 
+    @pl.when(first & has_low)
+    def _():
+        pl.semaphore_wait(low_ready, 1)
+        pp_low.start()
+        tile_low.start()
+        for q in range(4):
+            a_low[q].start()
+        one_low.start()
+
     def keep(i, k, value):
         prods[i, k] = value
 
@@ -336,22 +345,11 @@
     pl.when(has_left)(rel_left.start)
     pl.when(has_right)(rel_right.start)
     keep(1, 2, mul(a_raw[1, 2], pp_up[0]))
-    pl.when(has_low & ~first)(prod_low.start)
+    pl.when(has_low)(prod_low.start)
     pl.when(has_up)(tile_low.wait_recv)
-    pl.when(has_low & ~first)(tile_rel.start)
+    pl.when(has_low)(tile_rel.start)
     for r in range(2):
         transposed(2 + r, pp_up[r])
-
-    @pl.when(first & has_low)
-    def _():
-        pl.semaphore_wait(low_ready, 1)
-        pp_low.start()
-        tile_low.start()
-        for q in range(4):
-            a_low[q].start()
-        one_low.start()
-        prod_low.start()
-        tile_rel.start()
 
     def halo(q, xp, x_at, y_at, yp):
         pl.when(has_up)(a_low[q].wait_recv)
@@ -501,7 +499,7 @@
 
 
 def hand_over_kernel(blocks_hbm, numbers_hbm, out_hbm, out_numbers, held, in_sem, out_sem):
-    copies = [(r, slice(at, min(at + 3, SLOTS))) for r in range(2) for at in range(0, SLOTS, 3)]
+    copies = [(r, slice(at, at + 1)) for r in range(2) for at in range(SLOTS)]
     small = pltpu.make_async_copy(numbers_hbm, out_numbers, in_sem.at[len(copies)])
     small.start()
     reads = [
@@ -536,7 +534,7 @@
         out_specs=(any_, any_),
         scratch_shapes=[
             pltpu.VMEM((2, SLOTS, B, B), BF),
-            pltpu.SemaphoreType.DMA((13,)), pltpu.SemaphoreType.DMA((12,)),
+            pltpu.SemaphoreType.DMA((2 * SLOTS + 1,)), pltpu.SemaphoreType.DMA((2 * SLOTS,)),
         ],
         compiler_params=pltpu.CompilerParams(vmem_limit_bytes=VMEM_LIMIT),
     )(blocks, numbers)

time: 51.5 us -> 52.4 us (1.017)
  Pallas kernels: 50.6 us -> 51.5 us
    pallas_call x1, Pallas kernels: 2.9 us -> 3.77 us  [hand_over(): pl.pallas_call(hand_over_kernel, out_shape=(jax.ShapeDtypeStruct(blocks.s...]
where the time goes in v3:
time: 52.4 us; the launch traced here: 52.1 us
  Pallas kernels  51.5 us (98%)
  between operations  0.64 us (1%)
    pallas_call x1, Pallas kernels, gather_all(): pl.pallas_call(exchange_kernel, out_shape=(jax.ShapeDtypeStruct((2, SLOTS...  47.7 us
    pallas_call x1, Pallas kernels, hand_over(): pl.pallas_call(hand_over_kernel, out_shape=(jax.ShapeDtypeStruct(blocks.s...  3.77 us

profile of v3, /device:TPU:56, one launch (start us, length us, event | category | flops | bytes accessed | tf_op | source)
XLA Modules:
  0.0 52.1 jit_solution(16342903621059864882)
XLA Ops:
  0.6 47.7 %shard_map.50 = (bf16[2,17,192,192]{3,2,1,0:T(8,128)(2,1)}, s32[2]{0:T(128)}) custom-call(bf16[2,5,192,192]{3,2,1,0:T(8,128)(2,1)} %a_hbm.1, bf16[2,2,192,192]{3,2,1,0:T(8,128)(2,1)} %p_hbm.1, s32[2,2]{1,0:T(2,128)} %start_ref.1), custom_call_target="tpu_custom_call" | custom-call | tf_op jit(solution)/shard_map/pallas_call | solution.py:475
  48.4 3.8 %shard_map.51 = (bf16[2,17,192,192]{3,2,1,0:T(8,128)(2,1)}, s32[2]{0:T(128)}) custom-call(bf16[2,17,192,192]{3,2,1,0:T(8,128)(2,1)} %get-tuple-element.4.blocks_hbm, s32[2]{0:T(128)} %get-tuple-element.5.numbers_hbm), custom_call_target="tpu_custom_call" | custom-call | tf_op jit(solution)/shard_map/pallas_call | solution.py:527
